TPU v7x, 32 devices: a whole 2x2x4 slice. The times are simulated.
32 devices in a mesh: section: 4 (over z), row: 2 (over core), col: 4 (over y, x).
Axes of the slice: x: 2, y: 2, z: 4, core: 2. Of those that a mesh axis runs over, the one named last changes fastest.
Arguments:
- arriving: bfloat16 [4, 8, 16384], P('section', ('row', 'col')), may hold values from -64 to 64
- entering: bfloat16 [3, 8, 16384], P(None, ('row', 'col')), may hold values from -64 to 64
- gain: bfloat16 [4, 16384], P('section'), may hold values from 0.099609375 to 1.8984375
- kv_weight: bfloat16 [4, 16384, 1024], P('section', 'row', 'col'), may hold values from -0.046875 to 0.046875
- queries: bfloat16 [4, 4, 8, 8192], P('section', None, ('row', 'col')), may hold values from -150 to 150
- cache_keys: bfloat16 [4, 4, 8, 128, 512], P('section', None, ('row', 'col')), may hold values from -6 to 6
- cache_values: bfloat16 [4, 4, 8, 128, 512], P('section', None, ('row', 'col')), may hold values from -6 to 6
- lengths: int32 [7, 8], P(None, ('row', 'col')), may hold values from 2 to 128, as said below
Outputs:
- layer_out: bfloat16 [4, 4, 8, 16384], P('section', None, ('row', 'col'))
Inputs may be any that keep to these rules, and one draw needn't show every extreme that they name: Every row of lengths has a request with exactly 128 cached tokens, at a position drawn from the seed.
All inputs are finite; a program needn't handle non-finite values.
Results may differ from a plain program's by a relative error of at most 0.0034.
Values may be sent and summed in bfloat16 or wider, within the bound.
A program may use at most 64 MiB of HBM per device.

v0:
```python
import jax
import jax.numpy as jnp
import numpy as np
from jax import lax
from jax.sharding import PartitionSpec as P

QH = 64
KVH = 4
HD = 128


def shifted(array, axis, by):
    devices = lax.axis_size(axis)
    pairs = [(i, i + by) for i in range(devices) if 0 <= i + by < devices]
    return lax.ppermute(array, axis, pairs)


def rotate(keys, positions):
    half = HD // 2
    steps_up = jnp.arange(half).astype(jnp.float32)
    inverse = jnp.exp(-jnp.log(jnp.float32(500000.0)) * steps_up / half)
    angle = positions.astype(jnp.float32)[:, None] * inverse[None, :]
    cosine = jnp.cos(angle)[:, None, :]
    sine = jnp.sin(angle)[:, None, :]
    first = keys[..., :half]
    second = keys[..., half:]
    return jnp.concatenate(
        [first * cosine - second * sine, second * cosine + first * sine], axis=-1
    )


def attend(query_row, keys, values, new_key, new_value, length):
    slots = keys.shape[0]
    factor = 1.0 / np.sqrt(HD)
    grouped = query_row.reshape(KVH, QH // KVH, HD)
    cached = keys.reshape(slots, KVH, HD)
    stored = values.reshape(slots, KVH, HD)
    scores = (
        jnp.einsum("ghd,lgd->ghl", grouped, cached, preferred_element_type=jnp.float32) * factor
    )
    live = jnp.arange(slots) < length
    scores = jnp.where(live[None, None, :], scores, jnp.float32(-1e30))
    own = jnp.einsum("ghd,gd->gh", grouped, new_key, preferred_element_type=jnp.float32) * factor
    top = jnp.maximum(jnp.max(scores, axis=-1), own)
    weights = jnp.exp(scores - top[..., None])
    own_weight = jnp.exp(own - top)
    total = jnp.sum(weights, axis=-1) + own_weight
    probs = (weights / total[..., None]).astype(jnp.bfloat16)
    own_prob = (own_weight / total).astype(jnp.bfloat16)
    mixed = jnp.einsum("ghl,lgd->ghd", probs, stored, preferred_element_type=jnp.float32)
    mixed = (
        mixed + own_prob.astype(jnp.float32)[..., None] * new_value.astype(jnp.float32)[:, None, :]
    )
    return mixed.reshape(1, QH * HD)


def per_device(arriving, entering, gain, kv_weight, queries, cache_keys, cache_values, lengths):
    section_at = lax.axis_index("section")
    row_at = lax.axis_index("row")
    rows_count = lax.axis_size("row")
    cols_count = lax.axis_size("col")
    ticks = queries.shape[1]
    layers_all = lengths.shape[0] - ticks + 1
    width = arriving.shape[2]
    half_width = width // rows_count
    heads_width = QH * HD
    weight = kv_weight[0]
    gain_row = gain[0].astype(jnp.float32)
    current = arriving[0]
    outputs = []
    for tick in range(ticks):
        if tick > 0:
            passed = shifted(current, "section", 1)
            current = jnp.where(section_at == 0, entering[tick - 1], passed)
        length = lax.dynamic_index_in_dim(
            lengths[:, 0], tick - section_at + layers_all - 1, 0, keepdims=False
        )
        wide = current.astype(jnp.float32)
        scale = lax.rsqrt(jnp.mean(wide * wide, axis=1, keepdims=True) + 1e-05)
        normed = (wide * scale * gain_row[None, :]).astype(jnp.bfloat16)
        mine = lax.dynamic_slice_in_dim(
            lax.all_gather(normed, ("row", "col"), axis=0, tiled=True),
            row_at * half_width,
            half_width,
            1,
        )
        gathered = jnp.dot(mine, weight, preferred_element_type=jnp.float32)
        partial_rows = jnp.swapaxes(gathered.reshape(rows_count, cols_count, -1), 0, 1)
        summed = lax.psum_scatter(partial_rows, "row", scatter_dimension=1, tiled=True)
        fresh = lax.all_to_all(summed, "col", split_axis=0, concat_axis=2, tiled=True)
        fresh = fresh.reshape(KVH, 2, HD)
        new_key = rotate(fresh[None, :, 0, :], length[None])[0].astype(jnp.bfloat16)
        new_value = fresh[:, 1, :].astype(jnp.bfloat16)
        mixed = attend(
            queries[0, tick, 0],
            cache_keys[0, tick, 0],
            cache_values[0, tick, 0],
            new_key,
            new_value,
            length,
        )
        joined = jnp.concatenate([wide[:, :heads_width] + mixed, wide[:, heads_width:]], axis=1)
        current = joined.astype(jnp.bfloat16)
        outputs.append(current)
    return jnp.stack(outputs, axis=0)[None]


def solution(mesh):
    placed = (
        P("section", ("row", "col"), None),
        P(None, ("row", "col"), None),
        P("section", None),
        P("section", "row", "col"),
        P("section", None, ("row", "col"), None),
        P("section", None, ("row", "col"), None, None),
        P("section", None, ("row", "col"), None, None),
        P(None, ("row", "col")),
    )
    return jax.shard_map(
        per_device,
        mesh=mesh,
        in_specs=placed,
        out_specs=P("section", None, ("row", "col"), None),
        check_vma=False,
    )
```

profile of v0, /device:TPU:17, one launch (start us, length us, event | category | flops | bytes accessed | tf_op | source)
XLA Modules:
  0.0 192.7 jit_solution(15139149293575256739)
XLA Ops:
  0.0 1.7 multiply_reduce_fusion.3
  3.4 24.5 %all-gather = bf16[8,1,16384]{2,1,0:T(2,128)(2,1)S(1)} all-gather(bf16[1,1,16384]{2,1,0:T(2,128)(2,1)S(1)} %convert_bitcast_fusion.3), channel_id=1, replica_groups=mesh['section'=4,'row'=2,'col'=4] {'row','col'}, dimensions={0}, use_global_device_ids=true | all-gather | bytes 294912 | tf_op jit(solution)/shard_map/all_gather | solution.py:82
  28.7 2.9 %fusion.12 = f32[4,2,256]{2,0,1:T(4,128)S(1)} fusion(bf16[2,4,8192]{2,1,0:T(4,128)(2,1)S(1)} %dot_general.57, bf16[1,8192,256]{2,1,0:T(8,128)(2,1)} %param.11), kind=kOutput, calls=%fused_computation.20 | convolution fusion | flops 33554432 | bytes 4333568 | tf_op jit(solution)/shard_map/dot_general | solution.py:87
  31.6 3.1 %all-reduce = f32[4,2,256]{2,0,1:T(4,128)S(1)} all-reduce(f32[4,2,256]{2,0,1:T(4,128)S(1)} %fusion.12), channel_id=2, replica_groups=mesh['section'=4,'row'=2,'col'=4] {'row'}, use_global_device_ids=true, to_apply=%region_2.3.clone | all-reduce | flops 2048 | bytes 16384
  36.7 3.2 %all-to-all-start = ((f32[4,1,256]{2,1,0:T(1,128)}), f32[4,1,256]{2,1,0:T(1,128)S(1)}, u32[]{:S(2)}, u32[]{:S(2)}) async-start(f32[4,1,256]{2,1,0:T(1,128)} %copy.51), calls=%async_computation | async-start | bytes 8192 | tf_op jit(solution)/shard_map/all_to_all | solution.py:90
  47.5 3.2 %collective-permute-start = (bf16[1,16384]{1,0:T(2,128)(2,1)S(1)}, bf16[1,16384]{1,0:T(2,128)(2,1)S(1)}, u32[]{:S(2)}, u32[]{:S(2)}) collective-permute-start(bf16[1,16384]{1,0:T(2,128)(2,1)S(1)} %pad_maximum_fusion), channel_id=1, source_target_pairs={{0,8},{8,16},{16,24},{1,9},{9,17},{17,25},{2,10},{10,18},{18,26},{... | collective-permute-start | bytes 98312 | tf_op jit(solution)/shard_map/ppermute | solution.py:15
  54.0 26.1 %all-gather.1 = bf16[8,1,16384]{2,1,0:T(2,128)(2,1)S(1)} all-gather(bf16[1,1,16384]{2,1,0:T(2,128)(2,1)S(1)} %convert_bitcast_fusion.2), channel_id=1, replica_groups=mesh['section'=4,'row'=2,'col'=4] {'row','col'}, dimensions={0}, use_global_device_ids=true | all-gather | bytes 294912 | tf_op jit(solution)/shard_map/all_gather | solution.py:82
  81.0 2.9 %fusion.15 = f32[4,2,256]{2,0,1:T(4,128)S(1)} fusion(bf16[2,4,8192]{2,1,0:T(4,128)(2,1)S(1)} %dot_general.62, bf16[1,8192,256]{2,1,0:T(8,128)(2,1)} %param.11), kind=kOutput, calls=%fused_computation.21 | convolution fusion | flops 33554432 | bytes 4333568 | tf_op jit(solution)/shard_map/dot_general | solution.py:87
  83.9 3.0 %all-reduce.1 = f32[4,2,256]{2,0,1:T(4,128)S(1)} all-reduce(f32[4,2,256]{2,0,1:T(4,128)S(1)} %fusion.15), channel_id=3, replica_groups=mesh['section'=4,'row'=2,'col'=4] {'row'}, use_global_device_ids=true, to_apply=%region_6.7.clone | all-reduce | flops 2048 | bytes 16384
  88.2 3.2 %all-to-all-start.1 = ((f32[4,1,256]{2,1,0:T(1,128)}), f32[4,1,256]{2,1,0:T(1,128)S(1)}, u32[]{:S(2)}, u32[]{:S(2)}) async-start(f32[4,1,256]{2,1,0:T(1,128)} %copy.57), calls=%async_computation.1 | async-start | bytes 8192 | tf_op jit(solution)/shard_map/all_to_all | solution.py:90
  91.5 3.5 %all-to-all-done.1 = f32[4,1,256]{2,1,0:T(1,128)S(1)} async-done(((f32[4,1,256]{2,1,0:T(1,128)}), f32[4,1,256]{2,1,0:T(1,128)S(1)}, u32[]{:S(2)}, u32[]{:S(2)}) %all-to-all-start.1) | async-done | bytes 4128 | tf_op jit(solution)/shard_map/all_to_all | solution.py:90
  95.8 3.2 %collective-permute-start.1 = (bf16[1,16384]{1,0:T(2,128)(2,1)S(1)}, bf16[1,16384]{1,0:T(2,128)(2,1)S(1)}, u32[]{:S(2)}, u32[]{:S(2)}) collective-permute-start(bf16[1,16384]{1,0:T(2,128)(2,1)S(1)} %pad_maximum_fusion.1), channel_id=1, source_target_pairs={{0,8},{8,16},{16,24},{1,9},{9,17},{17,25},{2,10},{10,18},{18,26},{... | collective-permute-start | bytes 98312 | tf_op jit(solution)/shard_map/ppermute | solution.py:15
  102.3 26.4 %all-gather.2 = bf16[8,1,16384]{2,1,0:T(2,128)(2,1)S(1)} all-gather(bf16[1,1,16384]{2,1,0:T(2,128)(2,1)S(1)} %convert_bitcast_fusion.1), channel_id=1, replica_groups=mesh['section'=4,'row'=2,'col'=4] {'row','col'}, dimensions={0}, use_global_device_ids=true | all-gather | bytes 294912 | tf_op jit(solution)/shard_map/all_gather | solution.py:82
  129.5 2.9 %fusion.18 = f32[4,2,256]{2,0,1:T(4,128)S(1)} fusion(bf16[2,4,8192]{2,1,0:T(4,128)(2,1)S(1)} %dot_general.67, bf16[1,8192,256]{2,1,0:T(8,128)(2,1)} %param.11), kind=kOutput, calls=%fused_computation.22 | convolution fusion | flops 33554432 | bytes 4333568 | tf_op jit(solution)/shard_map/dot_general | solution.py:87
  132.4 2.5 %all-reduce.2 = f32[4,2,256]{2,0,1:T(4,128)S(1)} all-reduce(f32[4,2,256]{2,0,1:T(4,128)S(1)} %fusion.18), channel_id=4, replica_groups=mesh['section'=4,'row'=2,'col'=4] {'row'}, use_global_device_ids=true, to_apply=%region_10.11.clone | all-reduce | flops 2048 | bytes 16384
  136.3 3.2 %all-to-all-start.2 = ((f32[4,1,256]{2,1,0:T(1,128)}), f32[4,1,256]{2,1,0:T(1,128)S(1)}, u32[]{:S(2)}, u32[]{:S(2)}) async-start(f32[4,1,256]{2,1,0:T(1,128)} %copy.63), calls=%async_computation.2 | async-start | bytes 8192 | tf_op jit(solution)/shard_map/all_to_all | solution.py:90
  139.6 3.4 %all-to-all-done.2 = f32[4,1,256]{2,1,0:T(1,128)S(1)} async-done(((f32[4,1,256]{2,1,0:T(1,128)}), f32[4,1,256]{2,1,0:T(1,128)S(1)}, u32[]{:S(2)}, u32[]{:S(2)}) %all-to-all-start.2) | async-done | bytes 4128 | tf_op jit(solution)/shard_map/all_to_all | solution.py:90
  143.9 3.2 %collective-permute-start.2 = (bf16[1,16384]{1,0:T(2,128)(2,1)S(1)}, bf16[1,16384]{1,0:T(2,128)(2,1)S(1)}, u32[]{:S(2)}, u32[]{:S(2)}) collective-permute-start(bf16[1,16384]{1,0:T(2,128)(2,1)S(1)} %pad_maximum_fusion.2), channel_id=1, source_target_pairs={{0,8},{8,16},{16,24},{1,9},{9,17},{17,25},{2,10},{10,18},{18,26},{... | collective-permute-start | bytes 98312 | tf_op jit(solution)/shard_map/ppermute | solution.py:15
  147.2 1.6 collective-permute-done.2
  150.5 26.2 %all-gather.3 = bf16[8,1,16384]{2,1,0:T(2,128)(2,1)S(1)} all-gather(bf16[1,1,16384]{2,1,0:T(2,128)(2,1)S(1)} %convert_bitcast_fusion), channel_id=1, replica_groups=mesh['section'=4,'row'=2,'col'=4] {'row','col'}, dimensions={0}, use_global_device_ids=true | all-gather | bytes 294912 | tf_op jit(solution)/shard_map/all_gather | solution.py:82
  177.5 2.9 %fusion.21 = f32[4,2,256]{2,0,1:T(4,128)S(1)} fusion(bf16[2,4,8192]{2,1,0:T(4,128)(2,1)S(1)} %dot_general.72, bf16[1,8192,256]{2,1,0:T(8,128)(2,1)} %param.11), kind=kOutput, calls=%fused_computation.23 | convolution fusion | flops 33554432 | bytes 4333568 | tf_op jit(solution)/shard_map/dot_general | solution.py:87
  180.4 2.5 %all-reduce.3 = f32[4,2,256]{2,0,1:T(4,128)S(1)} all-reduce(f32[4,2,256]{2,0,1:T(4,128)S(1)} %fusion.21), channel_id=5, replica_groups=mesh['section'=4,'row'=2,'col'=4] {'row'}, use_global_device_ids=true, to_apply=%region_14.15.clone | all-reduce | flops 2048 | bytes 16384
  184.2 3.2 %all-to-all-start.3 = ((f32[4,1,256]{2,1,0:T(1,128)}), f32[4,1,256]{2,1,0:T(1,128)S(1)}, u32[]{:S(2)}, u32[]{:S(2)}) async-start(f32[4,1,256]{2,1,0:T(1,128)} %copy.69), calls=%async_computation.3 | async-start | bytes 8192 | tf_op jit(solution)/shard_map/all_to_all | solution.py:90
  187.5 3.4 %all-to-all-done.3 = f32[4,1,256]{2,1,0:T(1,128)S(1)} async-done(((f32[4,1,256]{2,1,0:T(1,128)}), f32[4,1,256]{2,1,0:T(1,128)S(1)}, u32[]{:S(2)}, u32[]{:S(2)}) %all-to-all-start.3) | async-done | bytes 4128 | tf_op jit(solution)/shard_map/all_to_all | solution.py:90
  (121 shorter events, 24.7 us)
Async XLA Ops:
  0.0 34.8 %copy-start.7 = (u32[32]{0:T(128)S(1)}, u32[32]{0:T(128)}, u32[]{:S(2)}) copy-start(u32[32]{0:T(128)} %constant.108) | copy-start | bytes 388
  0.0 40.0 %copy-start.1 = (bf16[1,1,16384]{2,1,0:T(2,128)(2,1)S(1)}, bf16[1,1,16384]{2,1,0:T(2,128)(2,1)}, u32[]{:S(2)}) copy-start(bf16[1,1,16384]{2,1,0:T(2,128)(2,1)} %param.8) | copy-start | bytes 98308
  0.0 40.1 %copy-start.6 = (s32[7,1]{0,1:T(1,128)S(1)}, s32[7,1]{0,1:T(1,128)}, u32[]{:S(2)}) copy-start(s32[7,1]{0,1:T(1,128)} %param.15) | copy-start | bytes 88
  0.0 43.8 %copy-start.5 = (bf16[1,4,1,8192]{3,1,2,0:T(4,128)(2,1)S(1)}, bf16[1,4,1,8192]{3,1,2,0:T(4,128)(2,1)}, u32[]{:S(2)}) copy-start(bf16[1,4,1,8192]{3,1,2,0:T(4,128)(2,1)} %param.12) | copy-start | bytes 196612
  0.0 44.2 %copy-start.2 = (bf16[1,4,1,128,512]{4,3,2,1,0:T(8,128)(2,1)S(1)}, bf16[1,4,1,128,512]{4,3,2,1,0:T(8,128)(2,1)}, u32[]{:S(2)}) copy-start(bf16[1,4,1,128,512]{4,3,2,1,0:T(8,128)(2,1)} %param.13) | copy-start | bytes 1572868
  28.6 16.1 %copy-start.3 = (bf16[1,4,1,128,512]{4,3,2,1,0:T(8,128)(2,1)S(1)}, bf16[1,4,1,128,512]{4,3,2,1,0:T(8,128)(2,1)}, u32[]{:S(2)}) copy-start(bf16[1,4,1,128,512]{4,3,2,1,0:T(8,128)(2,1)} %param.14) | copy-start | bytes 1572868
  31.6 20.9 %copy-start.4 = (bf16[3,1,16384]{2,0,1:T(4,128)(2,1)S(1)}, bf16[3,1,16384]{2,0,1:T(4,128)(2,1)}, u32[]{:S(2)}) copy-start(bf16[3,1,16384]{2,0,1:T(4,128)(2,1)} %param.9) | copy-start | bytes 294916
  31.6 22.4 %copy-start = (bf16[1,16384]{1,0:T(2,128)(2,1)S(1)}, bf16[1,16384]{1,0:T(2,128)(2,1)}, u32[]{:S(2)}) copy-start(bf16[1,16384]{1,0:T(2,128)(2,1)} %param.10) | copy-start | bytes 98308
  36.7 9.9 %all-to-all-start = ((f32[4,1,256]{2,1,0:T(1,128)}), f32[4,1,256]{2,1,0:T(1,128)S(1)}, u32[]{:S(2)}, u32[]{:S(2)}) async-start(f32[4,1,256]{2,1,0:T(1,128)} %copy.51), calls=%async_computation | async-start | bytes 8192 | tf_op jit(solution)/shard_map/all_to_all | solution.py:90
  47.5 5.0 %collective-permute-start = (bf16[1,16384]{1,0:T(2,128)(2,1)S(1)}, bf16[1,16384]{1,0:T(2,128)(2,1)S(1)}, u32[]{:S(2)}, u32[]{:S(2)}) collective-permute-start(bf16[1,16384]{1,0:T(2,128)(2,1)S(1)} %pad_maximum_fusion), channel_id=1, source_target_pairs={{0,8},{8,16},{16,24},{1,9},{9,17},{17,25},{2,10},{10,18},{18,26},{... | collective-permute-start | bytes 98312 | tf_op jit(solution)/shard_map/ppermute | solution.py:15
  88.2 6.8 %all-to-all-start.1 = ((f32[4,1,256]{2,1,0:T(1,128)}), f32[4,1,256]{2,1,0:T(1,128)S(1)}, u32[]{:S(2)}, u32[]{:S(2)}) async-start(f32[4,1,256]{2,1,0:T(1,128)} %copy.57), calls=%async_computation.1 | async-start | bytes 8192 | tf_op jit(solution)/shard_map/all_to_all | solution.py:90
  95.8 5.0 %collective-permute-start.1 = (bf16[1,16384]{1,0:T(2,128)(2,1)S(1)}, bf16[1,16384]{1,0:T(2,128)(2,1)S(1)}, u32[]{:S(2)}, u32[]{:S(2)}) collective-permute-start(bf16[1,16384]{1,0:T(2,128)(2,1)S(1)} %pad_maximum_fusion.1), channel_id=1, source_target_pairs={{0,8},{8,16},{16,24},{1,9},{9,17},{17,25},{2,10},{10,18},{18,26},{... | collective-permute-start | bytes 98312 | tf_op jit(solution)/shard_map/ppermute | solution.py:15
  136.3 6.7 %all-to-all-start.2 = ((f32[4,1,256]{2,1,0:T(1,128)}), f32[4,1,256]{2,1,0:T(1,128)S(1)}, u32[]{:S(2)}, u32[]{:S(2)}) async-start(f32[4,1,256]{2,1,0:T(1,128)} %copy.63), calls=%async_computation.2 | async-start | bytes 8192 | tf_op jit(solution)/shard_map/all_to_all | solution.py:90
  143.9 5.0 %collective-permute-start.2 = (bf16[1,16384]{1,0:T(2,128)(2,1)S(1)}, bf16[1,16384]{1,0:T(2,128)(2,1)S(1)}, u32[]{:S(2)}, u32[]{:S(2)}) collective-permute-start(bf16[1,16384]{1,0:T(2,128)(2,1)S(1)} %pad_maximum_fusion.2), channel_id=1, source_target_pairs={{0,8},{8,16},{16,24},{1,9},{9,17},{17,25},{2,10},{10,18},{18,26},{... | collective-permute-start | bytes 98312 | tf_op jit(solution)/shard_map/ppermute | solution.py:15
  184.2 6.7 %all-to-all-start.3 = ((f32[4,1,256]{2,1,0:T(1,128)}), f32[4,1,256]{2,1,0:T(1,128)S(1)}, u32[]{:S(2)}, u32[]{:S(2)}) async-start(f32[4,1,256]{2,1,0:T(1,128)} %copy.69), calls=%async_computation.3 | async-start | bytes 8192 | tf_op jit(solution)/shard_map/all_to_all | solution.py:90
where the time goes:
time: 195 us; the launch traced here: 193 us
  blocking collectives  114 us (58%)
  starting transfers between devices  22.6 us (12%)
  waiting for transfers between devices  14 us (7%)
  matrix products  13.9 us (7%)
  local copies, waits for them, and re-layouts  11.3 us (6%)
  other arithmetic  10.7 us (5%)
  between operations  5.78 us (3%)
    all_gather x4, blocking collectives, per_device(): lax.all_gather(normed, ('row', 'col'), axis=0, tiled=True)  103 us
    all_to_all x4, starting transfers between devices, per_device(): lax.all_to_all(summed, 'col', split_axis=0, concat_axis=2, tiled=True)  13 us
    dot_general x4, matrix products, per_device(): gathered = jnp.dot(mine, weight, preferred_element_type=jnp.float32)  11.5 us
    unnamed x4, blocking collectives  11.2 us
    all_to_all x4, waiting for transfers between devices, per_device(): lax.all_to_all(summed, 'col', split_axis=0, concat_axis=2, tiled=True)  10.4 us
    ppermute x3, starting transfers between devices, shifted(): return lax.ppermute(array, axis, pairs)  9.61 us
    unnamed x29, local copies, waits for them, and re-layouts  4.43 us
  transfers between devices with their start and end apart: 7, of which 6 were waited for; matrix products, arithmetic and copies ran while one was open for 3% of the time, Pallas kernels for 0%

commit v1 on v0

--- a/solution.py
+++ b/solution.py
@@ -1,12 +1,18 @@
+import functools
+
 import jax
 import jax.numpy as jnp
 import numpy as np
 from jax import lax
+from jax.experimental import pallas as pl
+from jax.experimental.pallas import tpu as pltpu
 from jax.sharding import PartitionSpec as P
 
 QH = 64
 KVH = 4
 HD = 128
+GROUP = QH // KVH
+MESH = pl.DeviceIdType.MESH
 
 
 def shifted(array, axis, by):
@@ -54,7 +60,7 @@
     return mixed.reshape(1, QH * HD)
 
 
-def per_device(arriving, entering, gain, kv_weight, queries, cache_keys, cache_values, lengths):
+def per_device_general(arriving, entering, gain, kv_weight, queries, cache_keys, cache_values, lengths):
     section_at = lax.axis_index("section")
     row_at = lax.axis_index("row")
     rows_count = lax.axis_size("row")
@@ -105,6 +111,342 @@
     return jnp.stack(outputs, axis=0)[None]
 
 
+def relay_kernel(
+    sections, ticks, cols, requests,
+    lens_ref, arr_ref, ent_ref, gain_ref, w_ref, q_ref, k_ref, v_ref, cs_ref,
+    out_ref,
+    wv, xj, xh, xs, qb_src, qb_buf, misc_src, misc_buf, p_src, p_buf, hj, lse_hj, xo, oj,
+    w_sem, send_sem, xj_sem, xh_sem, qb_sem, misc_sem, p_sem, z_sem, out_sem,
+):
+    f32, bf16 = jnp.float32, jnp.bfloat16
+    me_s, me_r, me_c = lax.axis_index("section"), lax.axis_index("row"), lax.axis_index("col")
+    me_j = me_r * cols + me_c
+    factor = 1.0 / np.sqrt(HD)
+    width = 2.0 * QH * HD
+    later = ticks - 1
+
+    def at(s, r, c):
+        return {"section": s, "row": r, "col": c}
+
+    barrier = pltpu.get_barrier_semaphore()
+
+    def greet(cond, where):
+        def do():
+            pl.semaphore_signal(barrier, inc=1, device_id=where, device_id_type=MESH)
+        if cond is True:
+            do()
+        else:
+            pl.when(cond)(do)
+
+    for dr in range(2):
+        for dc in range(cols):
+            if dr or dc:
+                greet(True, at(me_s, (me_r + dr) % 2, (me_c + dc) % cols))
+    for d in range(1, ticks):
+        greet(me_s >= d, at(me_s - d, me_r, me_c))
+    for dc in range(1, cols):
+        greet((me_r == 0) & (me_s >= 1), at(me_s - 1, me_r, (me_c + dc) % cols))
+
+    depth = w_ref.shape[0] // cols
+    def w_copy(b):
+        return pltpu.make_async_copy(
+            w_ref.at[pl.ds(b * depth, depth)], wv.at[pl.ds(b * depth, depth)], w_sem.at[b])
+    for b in range(cols):
+        w_copy(b).start()
+
+    out_ref[0, QH:] = arr_ref[QH:]
+    for t in range(1, ticks):
+        @pl.when(me_s < t)
+        def _():
+            out_ref[t, QH:] = ent_ref[t - 1 - me_s, QH:]
+
+    reach = jnp.minimum(ticks - 1, sections - 1 - me_s)
+    onward = jnp.where((me_r == 0) & (me_s + 1 < sections), cols - 1, 0)
+    pl.semaphore_wait(barrier, 2 * cols - 1 + reach + onward)
+
+    sent = []
+    on_chain, off_chain, has_next = me_r == 0, me_r == 1, me_s + 1 < sections
+    chain_next = on_chain & has_next
+
+    def remote(cond, src, dst, rsem, where, held=None, like=None):
+        number = len(sent)
+        sent.append((cond if held is None else held, (lambda: src) if like is None else like))
+
+        def go():
+            pltpu.make_async_remote_copy(
+                src_ref=src, dst_ref=dst, send_sem=send_sem.at[number], recv_sem=rsem,
+                device_id=where, device_id_type=MESH).start()
+        if cond is True:
+            go()
+        else:
+            pl.when(cond)(go)
+
+    def local(cond, src, dst, rsem):
+        def go():
+            pltpu.make_async_copy(src, dst, rsem).start()
+        pl.when(cond)(go)
+
+    def push(cond, src_of, dst, rsem, row):
+        for dc in range(cols):
+            col = (me_c + dc) % cols
+            if dc == 0:
+                here = me_r == row if cond is True else cond & (me_r == row)
+                away = me_r != row if cond is True else cond & (me_r != row)
+                local(here, src_of(col), dst, rsem)
+                remote(away, src_of(col), dst, rsem, at(me_s, row, col))
+            else:
+                remote(cond, src_of(col), dst, rsem, at(me_s, row, col))
+
+    def landed(ref, sem):
+        pltpu.make_async_copy(ref, ref, sem).wait()
+
+    def cache_part(t):
+        length = lens_ref[t]
+        lane = lax.broadcasted_iota(jnp.int32, (GROUP, HD), 1)
+        sub = lax.broadcasted_iota(jnp.int32, (GROUP, HD), 0)
+        lse_row = jnp.zeros((1, HD), f32)
+        for g in range(KVH):
+            qg = q_ref[t, g * GROUP:(g + 1) * GROUP, :]
+            kg = k_ref[t, :, g * HD:(g + 1) * HD]
+            vg = v_ref[t, :, g * HD:(g + 1) * HD]
+            s = lax.dot_general(qg, kg, (((1,), (1,)), ((), ())), preferred_element_type=f32) * factor
+            s = jnp.where(lane < length, s, f32(-1e30))
+            top = jnp.max(s, axis=1, keepdims=True)
+            e = jnp.exp(s - top)
+            total = jnp.sum(e, axis=1, keepdims=True)
+            base = jnp.dot((e / total).astype(bf16), vg, preferred_element_type=f32)
+            qb_src[g, t, :GROUP, :] = qg
+            qb_src[g, t, GROUP:, :] = base.astype(bf16)
+            lse = top + jnp.log(total)
+            lse_row += jnp.sum(jnp.where(lane == sub + g * GROUP, lse, 0.0), axis=0, keepdims=True)
+        misc_src[t * 8:t * 8 + 8, :] = cs_ref[t]
+        misc_src[t * 8 + 2:t * 8 + 3, :] = lse_row
+
+    def push_cache_part(first, count, number):
+        span = pl.ds(first, count)
+        push(True, lambda col: qb_src.at[col, span], qb_buf.at[me_j, span], qb_sem.at[number], 0)
+        push(True, lambda col: misc_src.at[pl.ds(first * 8, count * 8)],
+             misc_buf.at[me_j, pl.ds(first * 8, count * 8)], misc_sem.at[number], 0)
+
+    push(True, lambda col: arr_ref.at[pl.ds(0, QH)], xj.at[0, me_j], xj_sem.at[0], 0)
+    push(True, lambda col: arr_ref.at[pl.ds(QH, QH)], xj.at[0, me_j], xj_sem.at[0], 1)
+    for d in range(1, ticks):
+        remote(me_s + d < sections, arr_ref.at[pl.ds(QH, QH)], out_ref.at[d, pl.ds(QH, QH)],
+               z_sem.at[d], at(me_s + d, me_r, me_c))
+    for t in range(1, ticks):
+        push(me_s == 0, lambda col: ent_ref.at[t - 1, pl.ds(0, QH)], xj.at[t, me_j], xj_sem.at[t], 0)
+
+    cache_part(0)
+    push_cache_part(0, 1, 0)
+
+    def rest():
+        for t in range(1, ticks):
+            @pl.when(me_s >= t)
+            def _():
+                landed(out_ref.at[t, pl.ds(QH, QH)], z_sem.at[t])
+            push(True, lambda col: out_ref.at[t, pl.ds(QH, QH)], xj.at[t, me_j], xj_sem.at[t], 1)
+        for t in range(1, ticks):
+            cache_part(t)
+        push_cache_part(1, later, 1)
+
+    def turned(t):
+        return jnp.swapaxes(xj[t].astype(f32), 0, 1)
+
+    def lanes(x, gains, b):
+        parts = [x[h] * gains[h:h + 1] for h in range(b * GROUP, (b + 1) * GROUP)]
+        return jnp.concatenate(parts, axis=1)
+
+    def squares(x):
+        return jnp.sum(jnp.sum(x * x, axis=0), axis=1, keepdims=True)
+
+    def static_part(first, count):
+        gains = gain_ref[QH:].astype(f32)
+        for t in range(first, first + count):
+            landed(xj.at[t], xj_sem.at[t])
+        xt = [turned(t) for t in range(first, first + count)]
+        total = jnp.zeros((count * requests, 2 * HD), f32)
+        for b in range(cols):
+            lhs = jnp.concatenate([lanes(x, gains, b) for x in xt], axis=0).astype(bf16)
+            total += jnp.dot(lhs, wv[b * depth:(b + 1) * depth, :], preferred_element_type=f32)
+        for i in range(count):
+            p_src[first + i, :, :2 * HD] = total[i * requests:(i + 1) * requests]
+            p_src[first + i, :, 2 * HD:] = jnp.broadcast_to(squares(xt[i]), (requests, HD))
+
+    def prepare(t):
+        if t <= 1:
+            number, first, count = (0, 0, 1) if t == 0 else (1, 1, later)
+            landed(qb_buf.at[:, pl.ds(first, count)], qb_sem.at[number])
+            landed(misc_buf.at[:, pl.ds(first * 8, count * 8)], misc_sem.at[number])
+        hj[...] = jnp.swapaxes(qb_buf[:, t].astype(f32), 0, 1)
+        rows = jnp.concatenate([misc_buf[j, t * 8 + 2:t * 8 + 3, :] for j in range(requests)], axis=0)
+        lane = lax.broadcasted_iota(jnp.int32, (GROUP, requests, HD), 2)
+        head = lax.broadcasted_iota(jnp.int32, (GROUP, requests, HD), 0) + me_c * GROUP
+        picked = jnp.sum(jnp.where(lane == head, rows[None], 0.0), axis=2, keepdims=True)
+        lse_hj[...] = jnp.broadcast_to(picked, (GROUP, requests, HD))
+
+    def chain(t):
+        gains = gain_ref[:QH].astype(f32)
+        if t == 0:
+            landed(xj.at[0], xj_sem.at[0])
+            xs[...] = turned(0)
+        else:
+            @pl.when(me_s == 0)
+            def _():
+                landed(xj.at[t], xj_sem.at[t])
+                xs[...] = turned(t)
+
+            @pl.when(me_s > 0)
+            def _():
+                landed(xh.at[t - 1], xh_sem.at[t - 1])
+                xs[...] = xh[t - 1].astype(f32).reshape(QH, requests, HD)
+        x = xs[...]
+        fresh = jnp.zeros((requests, 2 * HD), f32)
+        for b in range(cols):
+            fresh += jnp.dot(lanes(x, gains, b).astype(bf16), wv[b * depth:(b + 1) * depth, :],
+                             preferred_element_type=f32)
+        power = squares(x)
+        if t <= 1:
+            span = pl.ds(0, 1) if t == 0 else pl.ds(1, later)
+            landed(p_buf.at[span], p_sem.at[t])
+        power += p_buf[t, :, 2 * HD:2 * HD + 1]
+        fresh = (fresh + p_buf[t, :, :2 * HD]) * lax.rsqrt(power / width + 1e-05)
+        cosine = jnp.concatenate([misc_buf[j, t * 8:t * 8 + 1, :] for j in range(requests)], axis=0)
+        sine = jnp.concatenate([misc_buf[j, t * 8 + 1:t * 8 + 2, :] for j in range(requests)], axis=0)
+        key = fresh[:, :HD]
+        key = key * cosine + pltpu.roll(key, HD // 2, 1) * sine
+        key = key.astype(bf16).astype(f32)
+        value = fresh[:, HD:].astype(bf16).astype(f32)
+        q = hj[:GROUP]
+        base = hj[GROUP:]
+        lse = lse_hj[...]
+        own = jnp.sum(q * key[None], axis=2, keepdims=True) * factor
+        top = jnp.maximum(lse, own)
+        old_weight = jnp.exp(lse - top)
+        own_weight = jnp.exp(own - top)
+        inverse = 1.0 / (old_weight + own_weight)
+        own_prob = (own_weight * inverse).astype(bf16).astype(f32)
+        mixed = base * (old_weight * inverse) + own_prob * value[None]
+        mine = xs[pl.ds(pl.multiple_of(me_c * GROUP, GROUP), GROUP)] + mixed
+        block = pl.ds(pl.multiple_of(me_c * GROUP, GROUP), GROUP)
+        if t + 1 < ticks:
+            rows = requests * GROUP
+            xo[t] = mine.reshape(rows, HD).astype(bf16)
+            for dc in range(cols):
+                remote(has_next, xo.at[t],
+                       xh.at[t, pl.ds(pl.multiple_of(me_c * rows, rows), rows)],
+                       xh_sem.at[t], at(me_s + 1, 0, (me_c + dc) % cols), held=chain_next, like=lambda: xo.at[t])
+        oj[t] = jnp.swapaxes(mine, 0, 1).astype(bf16)
+        for r in range(2):
+            for dc in range(cols):
+                col = (me_c + dc) % cols
+                src = oj.at[t, r * cols + col]
+                dst = out_ref.at[t, block]
+                if r == 0 and dc == 0:
+                    pltpu.make_async_copy(src, dst, out_sem.at[t]).start()
+                else:
+                    remote(True, src, dst, out_sem.at[t], at(me_s, r, col),
+                           held=on_chain, like=lambda: oj.at[t, 0])
+
+    def push_static(first, count):
+        span = pl.ds(first, count)
+        remote(True, p_src.at[span], p_buf.at[span], p_sem.at[0 if first == 0 else 1],
+               at(me_s, 0, me_c), held=off_chain, like=lambda: p_src.at[span])
+
+    for b in range(cols):
+        w_copy(b).wait()
+
+    @pl.when(me_r == 0)
+    def _():
+        prepare(0)
+        chain(0)
+
+    @pl.when(me_r == 1)
+    def _():
+        static_part(0, 1)
+        push_static(0, 1)
+
+    rest()
+
+    @pl.when(me_r == 1)
+    def _():
+        static_part(1, later)
+        push_static(1, later)
+
+    @pl.when(me_r == 0)
+    def _():
+        for t in range(1, ticks):
+            prepare(t)
+            chain(t)
+
+    for t in range(ticks):
+        landed(out_ref.at[t, pl.ds(0, QH)], out_sem.at[t])
+    for number, (cond, like) in enumerate(sent):
+        def done(number=number, like=like):
+            landed(like(), send_sem.at[number])
+        if cond is True:
+            done()
+        else:
+            pl.when(cond)(done)
+
+
+def per_device(arriving, entering, gain, kv_weight, queries, cache_keys, cache_values, lengths):
+    sections, cols = lax.axis_size("section"), lax.axis_size("col")
+    ticks = queries.shape[1]
+    requests = 2 * cols
+    layers_all = lengths.shape[0] - ticks + 1
+    start = layers_all - 1 - lax.axis_index("section")
+    lens = lax.dynamic_slice_in_dim(lengths[:, 0], start, ticks, 0)
+    half = HD // 2
+    inverse = jnp.exp(-jnp.log(jnp.float32(500000.0)) * jnp.arange(half).astype(jnp.float32) / half)
+    angle = lens.astype(jnp.float32)[:, None] * inverse[None, :]
+    cosine, sine = jnp.cos(angle), jnp.sin(angle)
+    turn = jnp.stack([jnp.concatenate([cosine, cosine], 1), jnp.concatenate([-sine, sine], 1)], axis=1)
+    turn = jnp.pad(turn, ((0, 0), (0, 6), (0, 0)))
+    blocks = arriving.shape[2] // HD
+    bf16, f32 = jnp.bfloat16, jnp.float32
+    vmem = pl.BlockSpec(memory_space=pltpu.VMEM)
+    dma = pltpu.SemaphoreType.DMA
+    out = pl.pallas_call(
+        functools.partial(relay_kernel, sections, ticks, cols, requests),
+        out_shape=jax.ShapeDtypeStruct((ticks, blocks, HD), bf16),
+        in_specs=[pl.BlockSpec(memory_space=pltpu.SMEM), vmem, vmem, vmem,
+                  pl.BlockSpec(memory_space=pl.ANY), vmem, vmem, vmem, vmem],
+        out_specs=vmem,
+        scratch_shapes=[
+            pltpu.VMEM(kv_weight.shape[1:], bf16),
+            pltpu.VMEM((ticks, requests, QH, HD), bf16),
+            pltpu.VMEM((ticks - 1, QH * requests, HD), bf16),
+            pltpu.VMEM((QH, requests, HD), f32),
+            pltpu.VMEM((KVH, ticks, 2 * GROUP, HD), bf16),
+            pltpu.VMEM((requests, ticks, 2 * GROUP, HD), bf16),
+            pltpu.VMEM((ticks * 8, HD), f32),
+            pltpu.VMEM((requests, ticks * 8, HD), f32),
+            pltpu.VMEM((ticks, requests, 3 * HD), f32),
+            pltpu.VMEM((ticks, requests, 3 * HD), f32),
+            pltpu.VMEM((2 * GROUP, requests, HD), f32),
+            pltpu.VMEM((GROUP, requests, HD), f32),
+            pltpu.VMEM((ticks - 1, requests * GROUP, HD), bf16),
+            pltpu.VMEM((ticks, requests, GROUP, HD), bf16),
+            dma((cols,)), dma((120,)), dma((ticks,)), dma((ticks - 1,)),
+            dma((2,)), dma((2,)), dma((2,)), dma((ticks,)), dma((ticks,)),
+        ],
+        compiler_params=pltpu.CompilerParams(
+            collective_id=0, has_side_effects=True, vmem_limit_bytes=40 * 1024 * 1024),
+        name="relay",
+    )(
+        lens,
+        arriving.reshape(blocks, HD),
+        entering.reshape(ticks - 1, blocks, HD),
+        gain.reshape(blocks, HD),
+        kv_weight[0],
+        queries.reshape(ticks, QH, HD),
+        cache_keys.reshape(ticks, *cache_keys.shape[3:]),
+        cache_values.reshape(ticks, *cache_values.shape[3:]),
+        turn,
+    )
+    return out.reshape(1, ticks, 1, blocks * HD)
+
+
 def solution(mesh):
     placed = (
         P("section", ("row", "col"), None),
@@ -116,10 +458,17 @@
         P("section", None, ("row", "col"), None, None),
         P(None, ("row", "col")),
     )
-    return jax.shard_map(
-        per_device,
-        mesh=mesh,
-        in_specs=placed,
-        out_specs=P("section", None, ("row", "col"), None),
-        check_vma=False,
-    )
+    fits = mesh.shape["col"] == KVH and mesh.shape["row"] == 2
+
+    def run(*args):
+        one_each = args[0].shape[1] == mesh.shape["row"] * mesh.shape["col"]
+        body = per_device if fits and one_each else per_device_general
+        return jax.shard_map(
+            body,
+            mesh=mesh,
+            in_specs=placed,
+            out_specs=P("section", None, ("row", "col"), None),
+            check_vma=False,
+        )(*args)
+
+    return run

time: 195 us -> 45.7 us (0.23)
  blocking collectives: 114 us -> 0 us
  Pallas kernels: 0 us -> 35.5 us
  starting transfers between devices: 22.6 us -> 0 us
  waiting for transfers between devices: 14 us -> 0 us
  matrix products: 13.9 us -> 0 us
  other arithmetic: 10.7 us -> 2.98 us
  between operations: 5.78 us -> 0.04 us
  local copies, waits for them, and re-layouts: 11.3 us -> 6.74 us
    all_gather x4 -> x0, blocking collectives: 103 us -> none  [per_device(): lax.all_gather(normed, ('row', 'col'), axis=0, tiled=True)]
    pallas_call x0 -> x1, Pallas kernels: none -> 35.5 us  [per_device(): pl.pallas_call(functools.partial(relay_kernel, sections, ticks, cols, req...]
    dot_general x16 -> x0, matrix products: 13.9 us -> none  [the longest x4 11.5 us: per_device(): gathered = jnp.dot(mine, weight, preferred_element_type=jnp.float32)]
    all_to_all x4 -> x0, starting transfers between devices: 13 us -> none  [per_device(): lax.all_to_all(summed, 'col', split_axis=0, concat_axis=2, tiled=True)]
    unnamed x4 -> x0, blocking collectives: 11.2 us -> none
    all_to_all x4 -> x0, waiting for transfers between devices: 10.4 us -> none  [per_device(): lax.all_to_all(summed, 'col', split_axis=0, concat_axis=2, tiled=True)]
    ppermute x3 -> x0, starting transfers between devices: 9.61 us -> none  [shifted(): return lax.ppermute(array, axis, pairs)]
    reduce_sum x8 -> x0, other arithmetic: 4.52 us -> none  [the longest x4 3.86 us: per_device(): scale = lax.rsqrt(jnp.mean(wide * wide, axis=1, keepdims=True) + 1e-05)]
  transfers between devices with their start and end apart: 7 -> 0, of which waited for: 6 -> 0; matrix products, arithmetic and copies ran while one was open for 3% -> 0% of each run, Pallas kernels for 0% -> 0%
where the time goes in v1:
time: 45.7 us; the launch traced here: 45.3 us
  Pallas kernels  35.5 us (78%)
  local copies, waits for them, and re-layouts  6.74 us (15%)
  other arithmetic  2.98 us (7%)
    pallas_call x1, Pallas kernels, per_device(): pl.pallas_call(functools.partial(relay_kernel, sections, ticks, cols, req...  35.5 us
    unnamed x8, local copies, waits for them, and re-layouts  6.04 us
    unnamed x2, other arithmetic  2.04 us

profile of v1, /device:TPU:17, one launch (start us, length us, event | category | flops | bytes accessed | tf_op | source)
XLA Modules:
  0.0 45.3 jit_solution(17761593336375360145)
XLA Ops:
  0.0 0.7 %convert_bitcast_fusion = (f32[4]{0:T(128)S(1)}, s32[4]{0:T(128)S(1)}) fusion(s32[7,1]{0,1:T(1,128)} %param.15, s32[]{:T(128)S(6)} %select_n.3), kind=kLoop, calls=%fused_computation.9 | loop fusion | flops 4 | bytes 52 | tf_op jit(solution)/shard_map/mul | solution.py:401
  0.7 0.1 multiply_cosine_fusion
  0.9 0.1 pad_maximum_fusion
  0.9 1.0 %reduce = bf16[16384]{0:T(1024)(128)(2,1)S(1)} reduce(bf16[1,1,16384]{2,1,0:T(2,128)(2,1)} %param.8, bf16[]{:T(256)} %constant.30), dimensions={0,1}, to_apply=%param.8.reduce_sub_computation | reduce | bytes 65538 | tf_op args[0]
  2.0 1.0 %reduce.1 = bf16[16384]{0:T(1024)(128)(2,1)S(1)} reduce(bf16[1,16384]{1,0:T(2,128)(2,1)} %param.10, bf16[]{:T(256)} %constant.30), dimensions={0}, to_apply=%param.10.reduce_sub_computation | reduce | bytes 65538 | tf_op args[2]
  3.0 0.9 %copy.15 = bf16[1,4,64,128]{3,2,1,0:T(8,128)(2,1)S(1)} copy(bf16[1,4,64,128]{3,1,2,0:T(4,128)(2,1)} %bitcast.33) | data formatting | bytes 131072
  3.8 0.9 %copy.14 = bf16[1,3,128,128]{3,2,1,0:T(8,128)(2,1)S(1)} copy(bf16[1,3,128,128]{3,1,2,0:T(4,128)(2,1)} %bitcast.32) | data formatting | bytes 196608
  4.8 0.0 copy-start
  4.8 2.2 %copy-done = bf16[1,8192,256]{2,1,0:T(8,128)(2,1)S(1)} copy-done((bf16[1,8192,256]{2,1,0:T(8,128)(2,1)S(1)}, bf16[1,8192,256]{2,1,0:T(8,128)(2,1)}, u32[]{:S(2)}) %copy-start) | copy-done | bytes 4194328
  7.0 0.0 copy-start.1
  7.0 1.0 %copy-done.1 = bf16[1,4,1,128,512]{4,3,2,1,0:T(8,128)(2,1)S(1)} copy-done((bf16[1,4,1,128,512]{4,3,2,1,0:T(8,128)(2,1)S(1)}, bf16[1,4,1,128,512]{4,3,2,1,0:T(8,128)(2,1)}, u32[]{:S(2)}) %copy-start.1) | copy-done | bytes 524312
  8.0 0.0 copy-start.2
  8.0 1.0 %copy-done.2 = bf16[1,4,1,128,512]{4,3,2,1,0:T(8,128)(2,1)S(1)} copy-done((bf16[1,4,1,128,512]{4,3,2,1,0:T(8,128)(2,1)S(1)}, bf16[1,4,1,128,512]{4,3,2,1,0:T(8,128)(2,1)}, u32[]{:S(2)}) %copy-start.2) | copy-done | bytes 524312
  9.0 35.5 %relay.1 = bf16[4,128,128]{2,1,0:T(8,128)(2,1)S(1)} custom-call(s32[4]{0:T(128)S(1)} %get-tuple-element.9.lens_ref, bf16[128,128]{1,0:T(8,128)(2,1)S(1)} %bitcast.30, bf16[3,128,128]{2,1,0:T(8,128)(2,1)S(1)} %bitcast.28, bf16[128,128]{1,0:T(8,128)(2,1)S(1)} %bitcast.31, bf16[8192,256]{1,0:T(8,128)(2,1)S(1)} %bitcast.25, bf16[4,64,128]{2,1,0:T(8,128)(2,1)S(1)} %bitcast.29, ...), custom_call_target="tpu_custom_call" | custom-call | tf_op jit(solution)/shard_map/relay/pallas_call | solution.py:409
  44.6 0.7 %reshape.34 = bf16[1,4,1,16384]{3,1,2,0:T(4,128)(2,1)} reshape(bf16[4,128,128]{2,1,0:T(8,128)(2,1)S(1)} %relay.1) | data formatting | bytes 262144 | tf_op jit(solution)/shard_map/reshape | solution.py:447
  (2 shorter events, 0.0 us)
Async XLA Ops:
  4.8 2.2 %copy-start = (bf16[1,8192,256]{2,1,0:T(8,128)(2,1)S(1)}, bf16[1,8192,256]{2,1,0:T(8,128)(2,1)}, u32[]{:S(2)}) copy-start(bf16[1,8192,256]{2,1,0:T(8,128)(2,1)} %param.11) | copy-start | bytes 12582916
  7.0 1.0 %copy-start.1 = (bf16[1,4,1,128,512]{4,3,2,1,0:T(8,128)(2,1)S(1)}, bf16[1,4,1,128,512]{4,3,2,1,0:T(8,128)(2,1)}, u32[]{:S(2)}) copy-start(bf16[1,4,1,128,512]{4,3,2,1,0:T(8,128)(2,1)} %param.13) | copy-start | bytes 1572868
  8.0 1.0 %copy-start.2 = (bf16[1,4,1,128,512]{4,3,2,1,0:T(8,128)(2,1)S(1)}, bf16[1,4,1,128,512]{4,3,2,1,0:T(8,128)(2,1)}, u32[]{:S(2)}) copy-start(bf16[1,4,1,128,512]{4,3,2,1,0:T(8,128)(2,1)} %param.14) | copy-start | bytes 1572868

commit v2 on v1

--- a/solution.py
+++ b/solution.py
@@ -113,10 +113,11 @@
 
 def relay_kernel(
     sections, ticks, cols, requests,
-    lens_ref, arr_ref, ent_ref, gain_ref, w_ref, q_ref, k_ref, v_ref, cs_ref,
+    lens_ref, arr_ref, ent_ref, gain_ref, w_ref, q_ref, k_ref, v_ref,
     out_ref,
-    wv, xj, xh, xs, qb_src, qb_buf, misc_src, misc_buf, p_src, p_buf, hj, lse_hj, xo, oj,
-    w_sem, send_sem, xj_sem, xh_sem, qb_sem, misc_sem, p_sem, z_sem, out_sem,
+    wv, kv, vv, rows_bf, gain_f, xj, xh, qb_src, qb_buf, misc_src, misc_buf, p_src, p_buf,
+    hj, lse_hj, xo, oj,
+    w_sem, k_sem, v_sem, send_sem, xj_sem, xh_sem, qb_sem, misc_sem, p_sem, z_sem, out_sem,
 ):
     f32, bf16 = jnp.float32, jnp.bfloat16
     me_s, me_r, me_c = lax.axis_index("section"), lax.axis_index("row"), lax.axis_index("col")
@@ -148,17 +149,39 @@
         greet((me_r == 0) & (me_s >= 1), at(me_s - 1, me_r, (me_c + dc) % cols))
 
     depth = w_ref.shape[0] // cols
+
+    def cache_copy(t):
+        return (pltpu.make_async_copy(k_ref.at[t], kv.at[t], k_sem.at[t]),
+                pltpu.make_async_copy(v_ref.at[t], vv.at[t], v_sem.at[t]))
+
     def w_copy(b):
-        return pltpu.make_async_copy(
-            w_ref.at[pl.ds(b * depth, depth)], wv.at[pl.ds(b * depth, depth)], w_sem.at[b])
+        span = pl.ds(b * depth, depth)
+        return pltpu.make_async_copy(w_ref.at[span], wv.at[span], w_sem.at[b])
+
+    for copy in cache_copy(0):
+        copy.start()
     for b in range(cols):
         w_copy(b).start()
-
-    out_ref[0, QH:] = arr_ref[QH:]
+    for t in range(1, ticks):
+        for copy in cache_copy(t):
+            copy.start()
+
+    def blocked(x):
+        count = x.shape[1] // HD
+        return jnp.swapaxes(jnp.stack([x[:, h * HD:(h + 1) * HD] for h in range(count)]), 0, 1)
+
+    held_rows = jnp.concatenate(
+        [arr_ref[...].astype(f32), ent_ref[...].astype(f32), gain_ref[...].astype(f32),
+         jnp.zeros((7 - ticks, arr_ref.shape[1]), f32)], axis=0)
+    held_rows = blocked(held_rows)
+    rows_bf[...] = held_rows[:ticks].astype(bf16)
+    gain_f[...] = held_rows[ticks]
+
+    out_ref[0, QH:] = rows_bf[0, QH:]
     for t in range(1, ticks):
         @pl.when(me_s < t)
         def _():
-            out_ref[t, QH:] = ent_ref[t - 1 - me_s, QH:]
+            out_ref[t, QH:] = rows_bf[t - me_s, QH:]
 
     reach = jnp.minimum(ticks - 1, sections - 1 - me_s)
     onward = jnp.where((me_r == 0) & (me_s + 1 < sections), cols - 1, 0)
@@ -200,15 +223,20 @@
     def landed(ref, sem):
         pltpu.make_async_copy(ref, ref, sem).wait()
 
+    def length_of(t):
+        return lens_ref[0, t - me_s + sections - 1]
+
     def cache_part(t):
-        length = lens_ref[t]
+        length = length_of(t)
+        for copy in cache_copy(t):
+            copy.wait()
         lane = lax.broadcasted_iota(jnp.int32, (GROUP, HD), 1)
         sub = lax.broadcasted_iota(jnp.int32, (GROUP, HD), 0)
         lse_row = jnp.zeros((1, HD), f32)
         for g in range(KVH):
-            qg = q_ref[t, g * GROUP:(g + 1) * GROUP, :]
-            kg = k_ref[t, :, g * HD:(g + 1) * HD]
-            vg = v_ref[t, :, g * HD:(g + 1) * HD]
+            qg = q_rows[t, g * GROUP:(g + 1) * GROUP, :].astype(bf16)
+            kg = kv[t, :, g * HD:(g + 1) * HD]
+            vg = vv[t, :, g * HD:(g + 1) * HD]
             s = lax.dot_general(qg, kg, (((1,), (1,)), ((), ())), preferred_element_type=f32) * factor
             s = jnp.where(lane < length, s, f32(-1e30))
             top = jnp.max(s, axis=1, keepdims=True)
@@ -219,8 +247,8 @@
             qb_src[g, t, GROUP:, :] = base.astype(bf16)
             lse = top + jnp.log(total)
             lse_row += jnp.sum(jnp.where(lane == sub + g * GROUP, lse, 0.0), axis=0, keepdims=True)
-        misc_src[t * 8:t * 8 + 8, :] = cs_ref[t]
-        misc_src[t * 8 + 2:t * 8 + 3, :] = lse_row
+        misc_src[t * 8:t * 8 + 8, :] = jnp.concatenate(
+            [cosines[t:t + 1], sines[t:t + 1], lse_row, jnp.zeros((5, HD), f32)], axis=0)
 
     def push_cache_part(first, count, number):
         span = pl.ds(first, count)
@@ -228,23 +256,36 @@
         push(True, lambda col: misc_src.at[pl.ds(first * 8, count * 8)],
              misc_buf.at[me_j, pl.ds(first * 8, count * 8)], misc_sem.at[number], 0)
 
-    push(True, lambda col: arr_ref.at[pl.ds(0, QH)], xj.at[0, me_j], xj_sem.at[0], 0)
-    push(True, lambda col: arr_ref.at[pl.ds(QH, QH)], xj.at[0, me_j], xj_sem.at[0], 1)
+    push(True, lambda col: rows_bf.at[0, pl.ds(QH, QH)], xj.at[0, me_j], xj_sem.at[0], 1)
+    push(True, lambda col: rows_bf.at[0, pl.ds(0, QH)], xj.at[0, me_j], xj_sem.at[0], 0)
     for d in range(1, ticks):
-        remote(me_s + d < sections, arr_ref.at[pl.ds(QH, QH)], out_ref.at[d, pl.ds(QH, QH)],
+        remote(me_s + d < sections, rows_bf.at[0, pl.ds(QH, QH)], out_ref.at[d, pl.ds(QH, QH)],
                z_sem.at[d], at(me_s + d, me_r, me_c))
-    for t in range(1, ticks):
-        push(me_s == 0, lambda col: ent_ref.at[t - 1, pl.ds(0, QH)], xj.at[t, me_j], xj_sem.at[t], 0)
+
+    half = HD // 2
+    tick_of = lax.broadcasted_iota(jnp.int32, (8, HD), 0)
+    lane_of = lax.broadcasted_iota(jnp.int32, (8, HD), 1)
+    step = jnp.where(lane_of < half, lane_of, lane_of - half).astype(f32)
+    place = jnp.zeros((8, HD), f32)
+    for t in range(ticks):
+        place = jnp.where(tick_of == t, length_of(t).astype(f32), place)
+    angle = place * jnp.exp(-jnp.log(f32(500000.0)) * step / half)
+    cosines = jnp.cos(angle)
+    sines = jnp.where(lane_of < half, -jnp.sin(angle), jnp.sin(angle))
+    q_rows = blocked(q_ref[...].astype(f32))
 
     cache_part(0)
     push_cache_part(0, 1, 0)
 
+    for t in range(1, ticks):
+        push(me_s == 0, lambda col: rows_bf.at[t, pl.ds(0, QH)], xj.at[t, me_j], xj_sem.at[t], 0)
+    for t in range(1, ticks):
+        @pl.when(me_s >= t)
+        def _():
+            landed(out_ref.at[t, pl.ds(QH, QH)], z_sem.at[t])
+        push(True, lambda col: out_ref.at[t, pl.ds(QH, QH)], xj.at[t, me_j], xj_sem.at[t], 1)
+
     def rest():
-        for t in range(1, ticks):
-            @pl.when(me_s >= t)
-            def _():
-                landed(out_ref.at[t, pl.ds(QH, QH)], z_sem.at[t])
-            push(True, lambda col: out_ref.at[t, pl.ds(QH, QH)], xj.at[t, me_j], xj_sem.at[t], 1)
         for t in range(1, ticks):
             cache_part(t)
         push_cache_part(1, later, 1)
@@ -252,59 +293,65 @@
     def turned(t):
         return jnp.swapaxes(xj[t].astype(f32), 0, 1)
 
-    def lanes(x, gains, b):
-        parts = [x[h] * gains[h:h + 1] for h in range(b * GROUP, (b + 1) * GROUP)]
-        return jnp.concatenate(parts, axis=1)
+    def lanes(x, gains):
+        return jnp.concatenate([x[h] * gains[h:h + 1] for h in range(GROUP)], axis=1)
 
     def squares(x):
         return jnp.sum(jnp.sum(x * x, axis=0), axis=1, keepdims=True)
 
     def static_part(first, count):
-        gains = gain_ref[QH:].astype(f32)
+        gains = gain_f[QH:]
         for t in range(first, first + count):
             landed(xj.at[t], xj_sem.at[t])
         xt = [turned(t) for t in range(first, first + count)]
         total = jnp.zeros((count * requests, 2 * HD), f32)
         for b in range(cols):
-            lhs = jnp.concatenate([lanes(x, gains, b) for x in xt], axis=0).astype(bf16)
+            heads = slice(b * GROUP, (b + 1) * GROUP)
+            lhs = jnp.concatenate([lanes(x[heads], gains[heads]) for x in xt], axis=0).astype(bf16)
             total += jnp.dot(lhs, wv[b * depth:(b + 1) * depth, :], preferred_element_type=f32)
         for i in range(count):
             p_src[first + i, :, :2 * HD] = total[i * requests:(i + 1) * requests]
             p_src[first + i, :, 2 * HD:] = jnp.broadcast_to(squares(xt[i]), (requests, HD))
 
+    rows = requests * GROUP
+
     def prepare(t):
+        def lay():
+            landed(xj.at[t], xj_sem.at[t])
+            xh[t] = turned(t).reshape(QH * requests, HD).astype(bf16)
+        if t == 0:
+            lay()
+        else:
+            pl.when(me_s == 0)(lay)
         if t <= 1:
             number, first, count = (0, 0, 1) if t == 0 else (1, 1, later)
             landed(qb_buf.at[:, pl.ds(first, count)], qb_sem.at[number])
             landed(misc_buf.at[:, pl.ds(first * 8, count * 8)], misc_sem.at[number])
         hj[...] = jnp.swapaxes(qb_buf[:, t].astype(f32), 0, 1)
-        rows = jnp.concatenate([misc_buf[j, t * 8 + 2:t * 8 + 3, :] for j in range(requests)], axis=0)
+        sums = jnp.concatenate([misc_buf[j, t * 8 + 2:t * 8 + 3, :] for j in range(requests)], axis=0)
         lane = lax.broadcasted_iota(jnp.int32, (GROUP, requests, HD), 2)
         head = lax.broadcasted_iota(jnp.int32, (GROUP, requests, HD), 0) + me_c * GROUP
-        picked = jnp.sum(jnp.where(lane == head, rows[None], 0.0), axis=2, keepdims=True)
+        picked = jnp.sum(jnp.where(lane == head, sums[None], 0.0), axis=2, keepdims=True)
         lse_hj[...] = jnp.broadcast_to(picked, (GROUP, requests, HD))
 
     def chain(t):
-        gains = gain_ref[:QH].astype(f32)
-        if t == 0:
-            landed(xj.at[0], xj_sem.at[0])
-            xs[...] = turned(0)
-        else:
-            @pl.when(me_s == 0)
-            def _():
-                landed(xj.at[t], xj_sem.at[t])
-                xs[...] = turned(t)
-
-            @pl.when(me_s > 0)
-            def _():
-                landed(xh.at[t - 1], xh_sem.at[t - 1])
-                xs[...] = xh[t - 1].astype(f32).reshape(QH, requests, HD)
-        x = xs[...]
         fresh = jnp.zeros((requests, 2 * HD), f32)
-        for b in range(cols):
-            fresh += jnp.dot(lanes(x, gains, b).astype(bf16), wv[b * depth:(b + 1) * depth, :],
+        power = jnp.zeros((requests, 1), f32)
+        own_rows = None
+        for k in range(cols):
+            b = (me_c + cols - k) % cols
+            span = pl.ds(pl.multiple_of(b * rows, rows), rows)
+            if t > 0:
+                @pl.when(me_s > 0)
+                def _():
+                    landed(xh.at[t, pl.ds(0, rows)], xh_sem.at[t - 1, k])
+            x = xh[t, span, :].astype(f32).reshape(GROUP, requests, HD)
+            own_rows = x if k == 0 else own_rows
+            gains = gain_f[pl.ds(pl.multiple_of(b * GROUP, GROUP), GROUP), :]
+            fresh += jnp.dot(lanes(x, gains).astype(bf16),
+                             wv[pl.ds(pl.multiple_of(b * depth, depth), depth), :],
                              preferred_element_type=f32)
-        power = squares(x)
+            power += squares(x)
         if t <= 1:
             span = pl.ds(0, 1) if t == 0 else pl.ds(1, later)
             landed(p_buf.at[span], p_sem.at[t])
@@ -326,15 +373,14 @@
         inverse = 1.0 / (old_weight + own_weight)
         own_prob = (own_weight * inverse).astype(bf16).astype(f32)
         mixed = base * (old_weight * inverse) + own_prob * value[None]
-        mine = xs[pl.ds(pl.multiple_of(me_c * GROUP, GROUP), GROUP)] + mixed
+        mine = own_rows + mixed
         block = pl.ds(pl.multiple_of(me_c * GROUP, GROUP), GROUP)
         if t + 1 < ticks:
-            rows = requests * GROUP
             xo[t] = mine.reshape(rows, HD).astype(bf16)
             for dc in range(cols):
                 remote(has_next, xo.at[t],
-                       xh.at[t, pl.ds(pl.multiple_of(me_c * rows, rows), rows)],
-                       xh_sem.at[t], at(me_s + 1, 0, (me_c + dc) % cols), held=chain_next, like=lambda: xo.at[t])
+                       xh.at[t + 1, pl.ds(pl.multiple_of(me_c * rows, rows), rows)],
+                       xh_sem.at[t, dc], at(me_s + 1, 0, (me_c + dc) % cols), held=chain_next, like=lambda: xo.at[t])
         oj[t] = jnp.swapaxes(mine, 0, 1).astype(bf16)
         for r in range(2):
             for dc in range(cols):
@@ -393,30 +439,24 @@
     sections, cols = lax.axis_size("section"), lax.axis_size("col")
     ticks = queries.shape[1]
     requests = 2 * cols
-    layers_all = lengths.shape[0] - ticks + 1
-    start = layers_all - 1 - lax.axis_index("section")
-    lens = lax.dynamic_slice_in_dim(lengths[:, 0], start, ticks, 0)
-    half = HD // 2
-    inverse = jnp.exp(-jnp.log(jnp.float32(500000.0)) * jnp.arange(half).astype(jnp.float32) / half)
-    angle = lens.astype(jnp.float32)[:, None] * inverse[None, :]
-    cosine, sine = jnp.cos(angle), jnp.sin(angle)
-    turn = jnp.stack([jnp.concatenate([cosine, cosine], 1), jnp.concatenate([-sine, sine], 1)], axis=1)
-    turn = jnp.pad(turn, ((0, 0), (0, 6), (0, 0)))
     blocks = arriving.shape[2] // HD
     bf16, f32 = jnp.bfloat16, jnp.float32
     vmem = pl.BlockSpec(memory_space=pltpu.VMEM)
+    hbm = pl.BlockSpec(memory_space=pltpu.HBM)
     dma = pltpu.SemaphoreType.DMA
     out = pl.pallas_call(
         functools.partial(relay_kernel, sections, ticks, cols, requests),
         out_shape=jax.ShapeDtypeStruct((ticks, blocks, HD), bf16),
-        in_specs=[pl.BlockSpec(memory_space=pltpu.SMEM), vmem, vmem, vmem,
-                  pl.BlockSpec(memory_space=pl.ANY), vmem, vmem, vmem, vmem],
+        in_specs=[pl.BlockSpec(memory_space=pltpu.SMEM), vmem, vmem, vmem, hbm, vmem, hbm, hbm],
         out_specs=vmem,
         scratch_shapes=[
             pltpu.VMEM(kv_weight.shape[1:], bf16),
+            pltpu.VMEM((ticks, *cache_keys.shape[3:]), bf16),
+            pltpu.VMEM((ticks, *cache_values.shape[3:]), bf16),
+            pltpu.VMEM((ticks, blocks, HD), bf16),
+            pltpu.VMEM((blocks, HD), f32),
             pltpu.VMEM((ticks, requests, QH, HD), bf16),
-            pltpu.VMEM((ticks - 1, QH * requests, HD), bf16),
-            pltpu.VMEM((QH, requests, HD), f32),
+            pltpu.VMEM((ticks, QH * requests, HD), bf16),
             pltpu.VMEM((KVH, ticks, 2 * GROUP, HD), bf16),
             pltpu.VMEM((requests, ticks, 2 * GROUP, HD), bf16),
             pltpu.VMEM((ticks * 8, HD), f32),
@@ -427,22 +467,22 @@
             pltpu.VMEM((GROUP, requests, HD), f32),
             pltpu.VMEM((ticks - 1, requests * GROUP, HD), bf16),
             pltpu.VMEM((ticks, requests, GROUP, HD), bf16),
-            dma((cols,)), dma((120,)), dma((ticks,)), dma((ticks - 1,)),
+            dma((cols,)), dma((ticks,)), dma((ticks,)), dma((120,)), dma((ticks,)),
+            dma((ticks - 1, cols)),
             dma((2,)), dma((2,)), dma((2,)), dma((ticks,)), dma((ticks,)),
         ],
         compiler_params=pltpu.CompilerParams(
-            collective_id=0, has_side_effects=True, vmem_limit_bytes=40 * 1024 * 1024),
+            collective_id=0, has_side_effects=True, vmem_limit_bytes=60 * 1024 * 1024),
         name="relay",
     )(
-        lens,
-        arriving.reshape(blocks, HD),
-        entering.reshape(ticks - 1, blocks, HD),
-        gain.reshape(blocks, HD),
+        lengths.reshape(1, -1),
+        arriving.reshape(1, -1),
+        entering.reshape(ticks - 1, -1),
+        gain,
         kv_weight[0],
-        queries.reshape(ticks, QH, HD),
+        queries.reshape(ticks, -1),
         cache_keys.reshape(ticks, *cache_keys.shape[3:]),
         cache_values.reshape(ticks, *cache_values.shape[3:]),
-        turn,
     )
     return out.reshape(1, ticks, 1, blocks * HD)
 

time: 45.7 us -> 37.7 us (0.82)
  local copies, waits for them, and re-layouts: 6.74 us -> 1.61 us
  other arithmetic: 2.98 us -> 0 us
  Pallas kernels: 35.5 us -> 36 us
    unnamed x8 -> x0, local copies, waits for them, and re-layouts: 6.04 us -> none
    unnamed x2 -> x0, other arithmetic: 2.04 us -> none
    reshape x1, local copies, waits for them, and re-layouts: 0.7 us -> 1.61 us  [per_device(): return out.reshape(1, ticks, 1, blocks * HD)]
    mul x1 -> x0, other arithmetic: 0.73 us -> none  [per_device(): angle = lens.astype(jnp.float32)[:, None] * inverse[None, :]]
where the time goes in v2:
time: 37.7 us; the launch traced here: 37.6 us
  Pallas kernels  36 us (95%)
  local copies, waits for them, and re-layouts  1.61 us (4%)
    pallas_call x1, Pallas kernels, per_device(): pl.pallas_call(functools.partial(relay_kernel, sections, ticks, cols, req...  36 us
    reshape x1, local copies, waits for them, and re-layouts, per_device(): return out.reshape(1, ticks, 1, blocks * HD)  1.61 us

profile of v2, /device:TPU:17, one launch (start us, length us, event | category | flops | bytes accessed | tf_op | source)
XLA Modules:
  0.0 37.6 jit_solution(14050026634686987381)
XLA Ops:
  0.0 36.0 %relay.1 = bf16[4,128,128]{2,1,0:T(8,128)(2,1)} custom-call(s32[1,7]{1,0:T(1,128)} %bitcast.13, bf16[1,16384]{1,0:T(2,128)(2,1)} %bitcast.11, bf16[3,16384]{1,0:T(4,128)(2,1)} %bitcast.10, bf16[1,16384]{1,0:T(2,128)(2,1)} %gain_ref.1, bf16[8192,256]{1,0:T(8,128)(2,1)} %bitcast.7, bf16[4,8192]{1,0:T(4,128)(2,1)} %bitcast.12, bf16[4,128,512]{2,1,0:T(8,128)(2,1)} %bitcast.8, ...), custom_call_target="tpu_custom_call" | custom-call | tf_op jit(solution)/shard_map/relay/pallas_call | solution.py:447
  36.0 1.6 %reshape.27 = bf16[1,4,1,16384]{3,1,2,0:T(4,128)(2,1)} reshape(bf16[4,128,128]{2,1,0:T(8,128)(2,1)} %relay.1) | data formatting | bytes 262144 | tf_op jit(solution)/shard_map/reshape | solution.py:487
